TPU v7x, 768 devices: a whole 4x8x12 slice. The times are simulated.
768 devices in a mesh: slab: 12 (over z), grp: 64 (over x, y, core).
Axes of the slice: x: 4, y: 8, z: 12, core: 2. Of those that a mesh axis runs over, the one named last changes fastest.
Arguments:
- coords: float32 [3, 6291456], P(None, ('slab', 'grp')), may hold values from -1 to 1
- charges: float32 [6291456], P(('slab', 'grp')), may hold values from -1.5 to 1.5
- multipoles: float32 [121, 393216], P(None, ('slab', 'grp')), may hold values from -6 to 6
- operators: float32 [8, 121, 121], replicated, may hold values from -0.5 to 0.5
- send_list: int32 [768, 1024], P(('slab', 'grp')), may hold values from 0 to 511
- near_list: int32 [393216, 8], P(('slab', 'grp')), may hold values from 0 to 1535
- m2l_source: int32 [768, 4096], P(('slab', 'grp')), may hold values from 0 to 1023
- m2l_target: int32 [768, 4096], P(('slab', 'grp')), may hold values from 0 to 512, as said below
- m2l_operator: int32 [768, 4096], P(('slab', 'grp')), may hold values from 0 to 7
Outputs:
- local_exp: float32 [121, 393216], P(None, ('slab', 'grp'))
- near_potential: float32 [6291456], P(('slab', 'grp'))
Inputs may be any that keep to these rules, and one draw needn't show every extreme that they name: `m2l_target`: entries past a block's count of used slots hold 512, an empty slot; the first block uses all 4096 slots.
All inputs are finite; a program needn't handle non-finite values.
Results may differ from a plain program's by a relative error of at most 0.00011.
Values sent between devices are 32-bit elements; how exact they have to be, the bound alone decides.
A program may use at most 64 MiB of HBM per device.

v0:
```python
import jax
import jax.numpy as jnp
from jax import lax
from jax.sharding import PartitionSpec as P

SOFT2 = 0.0625


def padded(cells, sides, width):
    for axis, dim in sides:
        count = lax.axis_size(axis)
        ends = count - 1
        head = lax.slice_in_dim(cells, 0, width, axis=dim)
        tail = lax.slice_in_dim(cells, cells.shape[dim] - width, cells.shape[dim], axis=dim)
        cells = jnp.concatenate(
            [
                lax.ppermute(tail, axis, [(i, (i + 1) % count) for i in range(ends)]),
                cells,
                lax.ppermute(head, axis, [((i + 1) % count, i) for i in range(ends)]),
            ],
            axis=dim,
        )
    return cells


def shards(
    coords,
    charges,
    multipoles,
    operators,
    send_list,
    near_list,
    m2l_source,
    m2l_target,
    m2l_operator,
):
    ncoef = multipoles.shape[0]
    leaves = multipoles.shape[1]
    npoints = charges.shape[0]
    per_leaf = npoints // leaves
    near_count = near_list.shape[1]
    stacked = jnp.concatenate([coords, charges[None, :]], axis=0)
    window = padded(stacked, (("slab", 1),), npoints)
    window_rows = jnp.transpose(window.reshape(4, 3 * leaves, per_leaf), (1, 0, 2)).reshape(
        3 * leaves, 4 * per_leaf
    )
    selector = (
        near_list.reshape(-1)[:, None] == jnp.arange(3 * leaves, dtype=jnp.int32)[None, :]
    ).astype(jnp.float32)
    picked = jnp.dot(selector, window_rows, precision=lax.Precision.HIGHEST)
    picked = picked.reshape(leaves, near_count, 4, per_leaf)
    sources = jnp.transpose(picked, (2, 0, 1, 3)).reshape(4, leaves, near_count * per_leaf)
    targets = jnp.transpose(stacked.reshape(4, leaves, per_leaf), (0, 2, 1))
    dx = targets[0][:, :, None] - sources[0][None]
    dy = targets[1][:, :, None] - sources[1][None]
    dz = targets[2][:, :, None] - sources[2][None]
    inverse = 1.0 / jnp.sqrt(dx * dx + dy * dy + dz * dz + SOFT2)
    potential = jnp.sum(inverse * sources[3][None], axis=2)
    near_potential = potential.T.reshape(npoints)
    outgoing = jnp.take(multipoles, send_list[0], axis=1)
    received = lax.all_to_all(outgoing, "grp", split_axis=1, concat_axis=1, tiled=True)
    columns_in = received.shape[1]
    op_count = operators.shape[0]
    table = jnp.einsum("ocd,de->coe", operators, received, precision=lax.Precision.HIGHEST)
    table = table.reshape(ncoef, op_count * columns_in)
    entry_index = m2l_operator[0] * columns_in + m2l_source[0]
    entry_columns = jnp.take(table, entry_index, axis=1)
    target_table = (m2l_target[0][:, None] == jnp.arange(leaves, dtype=jnp.int32)[None, :]).astype(
        jnp.float32
    )
    local_exp = jnp.dot(entry_columns, target_table, precision=lax.Precision.HIGHEST)
    return (local_exp, near_potential)


def solution(mesh):
    return jax.shard_map(
        shards,
        mesh=mesh,
        in_specs=(
            P(None, ("slab", "grp")),
            P(("slab", "grp")),
            P(None, ("slab", "grp")),
            P(),
            P(("slab", "grp"), None),
            P(("slab", "grp"), None),
            P(("slab", "grp"), None),
            P(("slab", "grp"), None),
            P(("slab", "grp"), None),
        ),
        out_specs=(P(None, ("slab", "grp")), P(("slab", "grp"))),
        check_vma=False,
    )
```

profile of v0, /device:TPU:1, one launch (start us, length us, event | category | flops | bytes accessed | tf_op | source)
XLA Modules:
  0.0 78.0 jit_solution(14058975560417093991)
XLA Ops:
  0.6 0.0 copy-start
  0.6 0.0 copy-start.2
  0.7 0.0 copy-start.1
  0.7 1.0 %pad_maximum_fusion.1 = f32[4,8192]{1,0:T(4,128)S(1)} fusion(f32[1,8192]{1,0:T(1,128)} %bitcast.60, f32[3,8192]{1,0:T(4,128)} %param.9), kind=kLoop, calls=%fused_computation.20 | loop fusion | flops 32768 | bytes 262144 | tf_op jit(solution)/shard_map/concatenate | solution.py:42
  1.7 1.3 %collective-permute-start.1 = (f32[4,8192]{1,0:T(4,128)S(1)}, f32[4,8192]{1,0:T(4,128)S(1)}, u32[]{:S(2)}, u32[]{:S(2)}) collective-permute-start(f32[4,8192]{1,0:T(4,128)S(1)} %pad_maximum_fusion.1), channel_id=1, source_target_pairs={{64,0},{128,64},{192,128},{256,192},{320,256},{384,320},{448,384},... | collective-permute-start | bytes 393224 | tf_op jit(solution)/shard_map/ppermute | solution.py:19
  3.0 5.5 %collective-permute-start = (f32[4,8192]{1,0:T(4,128)S(1)}, f32[4,8192]{1,0:T(4,128)S(1)}, u32[]{:S(2)}, u32[]{:S(2)}) collective-permute-start(f32[4,8192]{1,0:T(4,128)S(1)} %pad_maximum_fusion.1), channel_id=1, source_target_pairs={{0,64},{64,128},{128,192},{192,256},{256,320},{320,384},{384,448},... | collective-permute-start | bytes 393224 | tf_op jit(solution)/shard_map/ppermute | solution.py:17
  8.5 1.1 %copy.49 = f32[121,512]{0,1:T(8,128)S(1)} copy(f32[121,512]{1,0:T(8,128)} %param.11) | data formatting | bytes 495616 | tf_op args[2]
  9.6 0.0 copy-start.3
  9.6 0.0 copy-start.4
  9.6 0.7 compare_select_fusion.3
  10.3 0.5 broadcast.111
  10.8 1.3 %reduce.3 = s32[1024]{0:T(1024)S(1)} reduce(s32[1,1024]{1,0:T(1,128)} %param.13, s32[]{:T(128)} %broadcast.111), dimensions={0}, to_apply=%param.13.reduce_sub_computation.3 | reduce | bytes 8196 | tf_op args[4]
  12.2 0.1 squeeze.7
  12.3 2.8 %gather_fusion = f32[1024,121]{1,0:T(8,128)S(1)} fusion(f32[121,512]{0,1:T(8,128)S(1)} %copy.49, s32[1024]{0:T(1024)S(1)} %broadcast_clamp_fusion.1), kind=kCustom, calls=%fused_computation | custom fusion | bytes 995328 | tf_op jit(solution)/shard_map/jit(_take)/gather | solution.py:60
  15.1 1.0 %broadcast_select_fusion = f32[121,64,16]{0,2,1:T(8,128)} fusion(f32[121,64,16]{0,2,1:T(8,128)S(1)} %bitcast.55, pred[64,16]{1,0:T(8,128)(4,1)S(1)} %compare_and_fusion), kind=kLoop, calls=%fused_computation.18 | loop fusion | flops 123904 | bytes 992256 | tf_op jit(solution)/shard_map/jit(_take)/select_n | solution.py:60
  16.1 13.7 %all-to-all-start = ((f32[121,64,16]{0,2,1:T(8,128)}), f32[121,64,16]{0,2,1:T(8,128)S(1)}, u32[]{:S(2)}, u32[]{:S(2)}) async-start(f32[121,64,16]{0,2,1:T(8,128)} %broadcast_select_fusion), calls=%async_computation | async-start | bytes 1048576 | tf_op jit(solution)/shard_map/all_to_all | solution.py:61
  29.8 0.0 copy-done.2
  29.8 0.1 concatenate.14
  29.9 0.0 copy-done.1
  29.9 0.3 concatenate.13
  30.2 0.0 copy-done.3
  30.2 0.0 copy-done.4
  30.3 0.1 copy.52
  30.4 0.2 copy.51
  30.6 0.0 copy-start.5
  30.7 0.0 collective-permute-done.1
  30.7 0.0 collective-permute-done
  30.7 0.1 pad_maximum_fusion
  30.8 2.7 %reshape.143 = f32[4,1536,16]{2,1,0:T(8,128)} reshape(f32[4,24576]{1,0:T(4,128)S(1)} %pad_maximum_fusion) | data formatting | bytes 786432 | tf_op jit(solution)/shard_map/reshape | solution.py:44
  33.6 2.3 %copy.53 = f32[1536,4,16]{0,2,1:T(8,128)S(1)} copy(f32[1536,4,16]{2,0,1:T(8,128)} %bitcast.53) | data formatting | bytes 786432 | tf_op jit(solution)/shard_map/transpose | solution.py:44
  35.9 0.0 copy-done.5
  35.9 13.4 %fusion.7 = f32[4,512,8,16]{1,3,0,2:T(8,128)S(1)} fusion(s32[512,8]{0,1:T(8,128)S(1)} %copy-done.5, f32[1536,4,16]{0,2,1:T(8,128)S(1)} %copy.53), kind=kOutput, calls=%fused_computation.11 | convolution fusion | flops 4838129664 | bytes 1458176 | tf_op jit(solution)/shard_map/dot_general | solution.py:50
  49.3 0.1 fusion.16
  49.5 0.1 copy.57
  49.6 0.1 copy.56
  49.7 0.1 copy.55
  49.9 0.1 copy.54
  50.0 4.8 %multiply_reduce_fusion = f32[16,512]{1,0:T(8,128)S(1)} fusion(f32[512,128]{1,0:T(8,128)S(1)} %copy.57, f32[512,128]{1,0:T(8,128)S(1)} %copy.56, f32[16,512]{1,0:T(8,128)S(1)} %get-tuple-element.9, f32[512,128]{1,0:T(8,128)S(1)} %copy.55, f32[16,512]{1,0:T(8,128)S(1)} %get-tuple-element.10, f32[512,128]{1,0:T(8,128)S(1)} %copy.54, ...), kind=kLoop, calls=%fused_computation.8 | loop fusion | flops 11526144 | bytes 1179648 | tf_op jit(solution)/shard_map/reduce_sum | solution.py:58
  54.8 0.1 copy.58
  54.9 0.8 reshape.145
  55.6 0.0 all-to-all-done
  55.6 0.0 copy-done
  55.6 5.0 %fusion.12 = f32[1024,8,121]{2,0,1:T(8,128)} fusion(f32[121,1024,1]{0,1,2:T(8,128)S(1)} %bitcast.54, f32[8,121,121]{2,0,1:T(8,128)S(1)} %copy-done), kind=kOutput, calls=%fused_computation.14 | convolution fusion | flops 1439268864 | bytes 4929056 | tf_op jit(solution)/shard_map/ocd,de->coe/dot_general | solution.py:64
  60.6 0.0 copy-start.6
  60.6 13.0 %gather_fusion.1 = f32[4096,121]{1,0:T(8,128)S(1)} fusion(f32[121,8192]{0,1:T(8,128)} %bitcast.52, s32[4096]{0:T(1024)S(1)} %broadcast_clamp_fusion), kind=kCustom, calls=%fused_computation.1 | custom fusion | bytes 3981312 | tf_op jit(solution)/shard_map/jit(_take)/gather | solution.py:67
  73.6 0.0 copy-done.6
  73.6 4.4 %fusion.4 = f32[121,512]{1,0:T(8,128)} fusion(s32[4096]{0:T(1024)S(1)} %bitcast.66, f32[4096,121]{1,0:T(8,128)S(1)} %gather_fusion.1, pred[4096]{0:T(1024)(128)(4,1)S(1)} %compare_and_fusion.1), kind=kOutput, calls=%fused_computation.7 | convolution fusion | flops 3047657472 | bytes 2250752 | tf_op jit(solution)/shard_map/dot_general | solution.py:71
  (7 shorter events, 0.1 us)
Async XLA Ops:
  0.6 55.0 %copy-start = (f32[8,121,121]{2,0,1:T(8,128)S(1)}, f32[8,121,121]{2,0,1:T(8,128)}, u32[]{:S(2)}) copy-start(f32[8,121,121]{2,0,1:T(8,128)} %param.12) | copy-start | bytes 1405540
  0.6 29.1 %copy-start.2 = (f32[8192]{0:T(1024)S(1)}, f32[8192]{0:T(1024)}, u32[]{:S(2)}) copy-start(f32[8192]{0:T(1024)} %param.10) | copy-start | bytes 98308
  0.7 29.3 %copy-start.1 = (f32[3,8192]{1,0:T(4,128)S(1)}, f32[3,8192]{1,0:T(4,128)}, u32[]{:S(2)}) copy-start(f32[3,8192]{1,0:T(4,128)} %param.9) | copy-start | bytes 294916
  1.7 29.0 %collective-permute-start.1 = (f32[4,8192]{1,0:T(4,128)S(1)}, f32[4,8192]{1,0:T(4,128)S(1)}, u32[]{:S(2)}, u32[]{:S(2)}) collective-permute-start(f32[4,8192]{1,0:T(4,128)S(1)} %pad_maximum_fusion.1), channel_id=1, source_target_pairs={{64,0},{128,64},{192,128},{256,192},{320,256},{384,320},{448,384},... | collective-permute-start | bytes 393224 | tf_op jit(solution)/shard_map/ppermute | solution.py:19
  3.0 27.7 %collective-permute-start = (f32[4,8192]{1,0:T(4,128)S(1)}, f32[4,8192]{1,0:T(4,128)S(1)}, u32[]{:S(2)}, u32[]{:S(2)}) collective-permute-start(f32[4,8192]{1,0:T(4,128)S(1)} %pad_maximum_fusion.1), channel_id=1, source_target_pairs={{0,64},{64,128},{128,192},{192,256},{256,320},{320,384},{384,448},... | collective-permute-start | bytes 393224 | tf_op jit(solution)/shard_map/ppermute | solution.py:17
  9.6 20.6 %copy-start.3 = (s32[1,4096]{1,0:T(1,128)S(1)}, s32[1,4096]{1,0:T(1,128)}, u32[]{:S(2)}) copy-start(s32[1,4096]{1,0:T(1,128)} %param.15) | copy-start | bytes 49156
  9.6 20.6 %copy-start.4 = (s32[1,4096]{1,0:T(1,128)S(1)}, s32[1,4096]{1,0:T(1,128)}, u32[]{:S(2)}) copy-start(s32[1,4096]{1,0:T(1,128)} %param.17) | copy-start | bytes 49156
  16.1 39.6 %all-to-all-start = ((f32[121,64,16]{0,2,1:T(8,128)}), f32[121,64,16]{0,2,1:T(8,128)S(1)}, u32[]{:S(2)}, u32[]{:S(2)}) async-start(f32[121,64,16]{0,2,1:T(8,128)} %broadcast_select_fusion), calls=%async_computation | async-start | bytes 1048576 | tf_op jit(solution)/shard_map/all_to_all | solution.py:61
  30.6 5.3 %copy-start.5 = (s32[512,8]{0,1:T(8,128)S(1)}, s32[512,8]{0,1:T(8,128)}, u32[]{:S(2)}) copy-start(s32[512,8]{0,1:T(8,128)} %param.14) | copy-start | bytes 49156
  60.6 13.0 %copy-start.6 = (s32[1,4096]{1,0:T(1,128)S(1)}, s32[1,4096]{1,0:T(1,128)}, u32[]{:S(2)}) copy-start(s32[1,4096]{1,0:T(1,128)} %param.16) | copy-start | bytes 49156
where the time goes:
time: 78.4 us; the launch traced here: 78 us
  local copies, waits for them, and re-layouts  24.8 us (32%)
  matrix products  22.8 us (29%)
  starting transfers between devices  20.4 us (26%)
  other arithmetic  9.06 us (12%)
  between operations  0.93 us (1%)
    all_to_all x1, starting transfers between devices, shards(): lax.all_to_all(outgoing, 'grp', split_axis=1, concat_axis=1, tiled=True)  13.7 us
    dot_general x1, matrix products, shards(): picked = jnp.dot(selector, window_rows, precision=lax.Precision.HIGHEST)  13.4 us
    gather x1, local copies, waits for them, and re-layouts, shards(): entry_columns = jnp.take(table, entry_index, axis=1)  13 us
    ppermute x1, starting transfers between devices, padded(): lax.ppermute(tail, axis, [(i, (i + 1) % count) for i in range(ends)])  5.46 us
    dot_general x1, matrix products, shards(): jnp.einsum('ocd,de->coe', operators, received, precision=lax.Precision.HI...  4.99 us
    reduce_sum x1, other arithmetic, shards(): potential = jnp.sum(inverse * sources[3][None], axis=2)  4.75 us
    dot_general x1, matrix products, shards(): jnp.dot(entry_columns, target_table, precision=lax.Precision.HIGHEST)  4.4 us
    gather x1, local copies, waits for them, and re-layouts, shards(): outgoing = jnp.take(multipoles, send_list[0], axis=1)  2.81 us
  transfers between devices with their start and end apart: 3, of which 0 were waited for; matrix products, arithmetic and copies ran while one was open for 43% of the time, Pallas kernels for 0%

commit v1 on v0

v1 whole, which is shorter than its diff:
```python
import jax
import jax.numpy as jnp
from jax import lax
from jax.experimental import pallas as pl
from jax.experimental.pallas import tpu as pltpu
from jax.sharding import PartitionSpec as P

SOFT2 = 0.0625
F32, BF16, I32 = jnp.float32, jnp.bfloat16, jnp.int32


def split(x):
    high = x.astype(BF16)
    return high, (x - high.astype(F32)).astype(BF16)


def send_rows(mult_ref, send_ref, held, out_ref):
    held[...] = jnp.zeros_like(held)
    held[0:121, :] = mult_ref[...]
    high, low = split(held[...])
    both = jnp.concatenate([high, low], axis=0)
    for k in range(4):
        cols = slice(256 * k, 256 * k + 256)
        pick = (lax.broadcasted_iota(I32, (512, 256), 0) == send_ref[:, cols]).astype(BF16)
        got = jnp.dot(both, pick, preferred_element_type=F32)
        out_ref[cols, :] = (got[:128] + got[128:]).T


def own_window(coords_ref, charges_ref, stage, own):
    for c in range(64):
        for q in range(3):
            stage[q // 2, pl.ds(64 * (q % 2) + c, 1), :] = coords_ref[q : q + 1, 128 * c : 128 * c + 128]
    stage[1, 64:128, :] = charges_ref[...]
    lane = lax.broadcasted_iota(I32, (16, 128), 1)
    for h in range(2):
        t = stage[h].T
        for j in range(4):
            left, right = t[32 * j : 32 * j + 16], t[32 * j + 16 : 32 * j + 32]
            own[j, 32 * h : 32 * h + 16, :] = jnp.where(lane < 64, left, pltpu.roll(right, 64, 1))
            own[j, 32 * h + 16 : 32 * h + 32, :] = jnp.where(lane < 64, pltpu.roll(left, 64, 1), right)


def take(x, index):
    return jnp.take_along_axis(x, index, axis=1)


def near_index(near_ref, tile_ref, lane_ref):
    lane = lax.broadcasted_iota(I32, (8, 128), 1)
    c, half = lane & 63, lane >> 6
    for j in range(4):
        spot = 8 * (c & 15) + 2 * j + half
        w = jnp.zeros((8, 128), I32)
        for k in range(4):
            w = jnp.where((c >> 4) == k, take(near_ref[:, 128 * k : 128 * k + 128], spot), w)
        leaf = w & 511
        tile_ref[j] = (w >> 9) * 4 + ((leaf & 7) >> 1)
        lane_ref[j] = (leaf & 1) * 64 + (leaf >> 3)


def near_gather(window, tile_ref, lane_ref, sources):
    def body(step, carry):
        j, n = step // 8, step % 8
        tile = jnp.broadcast_to(tile_ref[j, pl.ds(n, 1), :], (8, 128))
        spot = jnp.broadcast_to(lane_ref[j, pl.ds(n, 1), :], (8, 128))
        masks = [tile == k for k in range(12)]
        for r in range(8):
            rows = slice(8 * r, 8 * r + 8)
            got = take(window[0, rows, :], spot)
            for k in range(1, 12):
                got = jnp.where(masks[k], take(window[k, rows, :], spot), got)
            sources[j, n, rows, :] = got
        return carry

    lax.fori_loop(0, 32, body, 0)


def near_sum(own, sources, pot):
    def body(step, carry):
        j, i = step // 8, step % 8
        targets = [
            [jnp.broadcast_to(own[j, pl.ds(16 * q + i + 8 * u, 1), :], (8, 128)) for q in range(3)]
            for u in range(2)
        ]
        total = [jnp.zeros((8, 128), F32) for _ in range(2)]
        for n in range(8):
            for h in range(2):
                s = [sources[j, n, 16 * q + 8 * h : 16 * q + 8 * h + 8, :] for q in range(4)]
                for u in range(2):
                    dx, dy, dz = (targets[u][q] - s[q] for q in range(3))
                    total[u] = total[u] + s[3] * lax.rsqrt(dx * dx + dy * dy + dz * dz + SOFT2)
        for u in range(2):
            pot[j, pl.ds(i + 8 * u, 1), :] = jnp.sum(total[u], axis=0, keepdims=True)
        return carry

    lax.fori_loop(0, 32, body, 0)


def near_out(pot, flip, out_ref):
    for j in range(4):
        flip[32 * j : 32 * j + 16, :] = pot[j]
        flip[32 * j + 16 : 32 * j + 32, :] = pltpu.roll(pot[j], 64, 1)
    out_ref[...] = flip[...].T[0:64]


def operator_parts(ops_ref, pad, first, second):
    pad[...] = jnp.zeros_like(pad)
    for o in range(8):
        pad[0:121, 0:121] = ops_ref[:, o, :]
        high, low = split(pad[...])
        rows = slice(128 * (o % 2), 128 * (o % 2) + 128)
        first[o // 2, rows, 0:128] = high
        first[o // 2, rows, 128:256] = high
        second[o // 2, rows, :] = low


NT = (((1,), (1,)), ((), ()))


def translate(rows, first, second, table, start):
    count = rows.shape[0]
    high, low = split(rows)
    both = jnp.concatenate([high, low], axis=1)
    for k in range(4):
        got = lax.dot_general(both, first[k], NT, preferred_element_type=F32)
        got = got + lax.dot_general(high, second[k], NT, preferred_element_type=F32)
        table[pl.ds(2 * k * 1024 + start, count), :] = got[:, :128]
        table[pl.ds((2 * k + 1) * 1024 + start, count), :] = got[:, 128:]


def target_table(target_ref, hot):
    for k in range(16):
        cols = slice(256 * k, 256 * k + 256)
        hot[:, cols] = (lax.broadcasted_iota(I32, (512, 256), 0) == target_ref[:, cols]).astype(BF16)


def collect(index_ref, table, picked):
    def body(step, carry):
        base = step * 64
        for u in range(64):
            picked[pl.ds(base + u, 1), :] = table[pl.ds(index_ref[0, base + u], 1), :]
        return carry

    lax.fori_loop(0, 64, body, 0)


def gather_sum(hot, picked, total):
    total[...] = jnp.zeros_like(total)
    for k in range(8):
        rows = slice(512 * k, 512 * k + 512)
        high, low = split(picked[rows, :])
        both = jnp.concatenate([high, low], axis=1)
        total[...] += jnp.dot(hot[:, rows], both, preferred_element_type=F32)


def far_out(total, out_ref):
    for j in range(4):
        rows = slice(128 * j, 128 * j + 128)
        out_ref[:, rows] = (total[rows, :128] + total[rows, 128:]).T[0:121]


MESH = pl.DeviceIdType.MESH


def kernel(
    index_ref,
    coords_ref,
    charges_ref,
    mult_ref,
    ops_ref,
    send_ref,
    near_ref,
    target_ref,
    far_ref,
    pot_ref,
    stage,
    window,
    tile,
    spot,
    sources,
    pot,
    flip,
    held,
    outgoing,
    received,
    pad,
    first,
    second,
    table,
    hot,
    picked,
    total,
    halo_send,
    halo_recv,
    rows_send,
    rows_recv,
):
    slabs, groups = lax.axis_size("slab"), lax.axis_size("grp")
    s, g = lax.axis_index("slab"), lax.axis_index("grp")

    barrier = pltpu.get_barrier_semaphore()

    def greet(d, carry):
        other = lax.rem(g + d, groups)
        pl.semaphore_signal(barrier, inc=1, device_id={"grp": other}, device_id_type=MESH)
        return carry

    lax.fori_loop(1, groups, greet, 0)

    @pl.when(s > 0)
    def _():
        pl.semaphore_signal(barrier, inc=1, device_id={"slab": s - 1}, device_id_type=MESH)

    @pl.when(s < slabs - 1)
    def _():
        pl.semaphore_signal(barrier, inc=1, device_id={"slab": s + 1}, device_id_type=MESH)

    send_rows(mult_ref, send_ref, held, outgoing)
    own = window.at[4:8]
    own_window(coords_ref, charges_ref, stage, own)

    inner = jnp.where(s > 0, 1, 0) + jnp.where(s < slabs - 1, 1, 0)
    pl.semaphore_wait(barrier, groups - 1 + inner)

    def rows_copy(other):
        return pltpu.make_async_remote_copy(
            src_ref=outgoing.at[pl.ds(pl.multiple_of(16 * other, 16), 16)],
            dst_ref=received.at[pl.ds(pl.multiple_of(16 * g, 16), 16)],
            send_sem=rows_send,
            recv_sem=rows_recv.at[g // 8],
            device_id={"grp": other},
            device_id_type=MESH,
        )

    up = pltpu.make_async_remote_copy(
        src_ref=own,
        dst_ref=window.at[0:4],
        send_sem=halo_send.at[0],
        recv_sem=halo_recv.at[0],
        device_id={"slab": jnp.minimum(s + 1, slabs - 1)},
        device_id_type=MESH,
    )
    down = pltpu.make_async_remote_copy(
        src_ref=own,
        dst_ref=window.at[8:12],
        send_sem=halo_send.at[1],
        recv_sem=halo_recv.at[1],
        device_id={"slab": jnp.maximum(s - 1, 0)},
        device_id_type=MESH,
    )

    @pl.when(s < slabs - 1)
    def _():
        up.start()

    @pl.when(s > 0)
    def _():
        down.start()

    def send(d, carry):
        rows_copy(lax.rem(g + d, groups)).start()
        return carry

    lax.fori_loop(1, groups, send, 0)

    mine = pl.ds(pl.multiple_of(16 * g, 16), 16)
    received[mine, :] = outgoing[mine, :]

    near_index(near_ref, tile, spot)
    operator_parts(ops_ref, pad, first, second)
    target_table(target_ref, hot)

    @pl.when(s == 0)
    def _():
        window[0:4] = jnp.zeros((4, 64, 128), F32)

    @pl.when(s == slabs - 1)
    def _():
        window[8:12] = jnp.zeros((4, 64, 128), F32)

    @pl.when(s > 0)
    def _():
        up.wait_recv()

    @pl.when(s < slabs - 1)
    def _():
        down.wait_recv()

    near_gather(window, tile, spot, sources)
    near_sum(own, sources, pot)
    near_out(pot, flip, pot_ref)

    def arrived(count, k):
        block = pl.ds(0, 16 * count)
        return pltpu.make_async_remote_copy(
            src_ref=outgoing.at[block],
            dst_ref=received.at[block],
            send_sem=rows_send,
            recv_sem=rows_recv.at[k],
            device_id={"grp": lax.rem(g + 1, groups)},
            device_id_type=MESH,
        )

    for k in range(groups // 8):

        @pl.when(g // 8 == k)
        def _():
            arrived(7, k).wait_recv()

        @pl.when(g // 8 != k)
        def _():
            arrived(8, k).wait_recv()

        translate(received[128 * k : 128 * k + 128, :], first, second, table, 128 * k)

    collect(index_ref, table, picked)
    gather_sum(hot, picked, total)
    far_out(total, far_ref)

    arrived(groups - 1, 0).wait_send()

    @pl.when(s < slabs - 1)
    def _():
        up.wait_send()

    @pl.when(s > 0)
    def _():
        down.wait_send()


def shards(
    coords,
    charges,
    multipoles,
    operators,
    send_list,
    near_list,
    m2l_source,
    m2l_target,
    m2l_operator,
):
    index = m2l_operator * 1024 + m2l_source
    vmem = pl.BlockSpec(memory_space=pltpu.VMEM)
    far, pot = pl.pallas_call(
        kernel,
        out_shape=[jax.ShapeDtypeStruct((121, 512), F32), jax.ShapeDtypeStruct((64, 128), F32)],
        in_specs=[pl.BlockSpec(memory_space=pltpu.SMEM)] + [vmem] * 7,
        out_specs=[vmem, vmem],
        scratch_shapes=[
            pltpu.VMEM((2, 128, 128), F32),
            pltpu.VMEM((12, 64, 128), F32),
            pltpu.VMEM((4, 8, 128), I32),
            pltpu.VMEM((4, 8, 128), I32),
            pltpu.VMEM((4, 8, 64, 128), F32),
            pltpu.VMEM((4, 16, 128), F32),
            pltpu.VMEM((128, 128), F32),
            pltpu.VMEM((128, 512), F32),
            pltpu.VMEM((1024, 128), F32),
            pltpu.VMEM((1024, 128), F32),
            pltpu.VMEM((128, 128), F32),
            pltpu.VMEM((4, 256, 256), BF16),
            pltpu.VMEM((4, 256, 128), BF16),
            pltpu.VMEM((8192, 128), F32),
            pltpu.VMEM((512, 4096), BF16),
            pltpu.VMEM((4096, 128), F32),
            pltpu.VMEM((512, 256), F32),
            pltpu.SemaphoreType.DMA((2,)),
            pltpu.SemaphoreType.DMA((2,)),
            pltpu.SemaphoreType.DMA,
            pltpu.SemaphoreType.DMA((8,)),
        ],
        compiler_params=pltpu.CompilerParams(
            collective_id=0, has_side_effects=True, vmem_limit_bytes=40 * 2**20
        ),
    )(
        index,
        coords,
        charges.reshape(64, 128),
        multipoles,
        jnp.transpose(operators, (1, 0, 2)),
        send_list,
        near_list.T,
        m2l_target,
    )
    return far, pot.reshape(-1)


def solution(mesh):
    both = ("slab", "grp")
    return jax.shard_map(
        shards,
        mesh=mesh,
        in_specs=(P(None, both), P(both), P(None, both), P()) + (P(both, None),) * 5,
        out_specs=(P(None, both), P(both)),
        check_vma=False,
    )
```

time: 78.4 us -> 44.1 us (0.56)
  Pallas kernels: 0 us -> 37.3 us
  matrix products: 22.8 us -> 0 us
  starting transfers between devices: 20.4 us -> 0 us
  local copies, waits for them, and re-layouts: 24.8 us -> 4.93 us
  other arithmetic: 9.06 us -> 0.77 us
    pallas_call x0 -> x1, Pallas kernels: none -> 37.3 us  [shards(): pl.pallas_call(kernel, out_shape=[jax.ShapeDtypeStruct((121, 512), F32),...]
    dot_general x3 -> x0, matrix products: 22.8 us -> none  [the longest x1 13.4 us: shards(): picked = jnp.dot(selector, window_rows, precision=lax.Precision.HIGHEST)]
    gather x2 -> x0, local copies, waits for them, and re-layouts: 15.8 us -> none  [the longest x1 13 us: shards(): entry_columns = jnp.take(table, entry_index, axis=1)]
    all_to_all x1 -> x0, starting transfers between devices: 13.7 us -> none  [shards(): lax.all_to_all(outgoing, 'grp', split_axis=1, concat_axis=1, tiled=True)]
    ppermute x2 -> x0, starting transfers between devices: 6.75 us -> none  [the longest x1 5.46 us: padded(): lax.ppermute(tail, axis, [(i, (i + 1) % count) for i in range(ends)])]
    reduce_sum x1 -> x0, other arithmetic: 4.75 us -> none  [shards(): potential = jnp.sum(inverse * sources[3][None], axis=2)]
    reshape x2 -> x0, local copies, waits for them, and re-layouts: 3.5 us -> none  [the longest x1 2.75 us: shards(): window.reshape(4, 3 * leaves, per_leaf)]
    unnamed x16, local copies, waits for them, and re-layouts: 1.63 us -> 4.93 us
  transfers between devices with their start and end apart: 3 -> 0, of which waited for: 0 -> 0; matrix products, arithmetic and copies ran while one was open for 43% -> 0% of each run, Pallas kernels for 0% -> 0%
where the time goes in v1:
time: 44.1 us; the launch traced here: 43.7 us
  Pallas kernels  37.3 us (85%)
  local copies, waits for them, and re-layouts  4.93 us (11%)
  other arithmetic  0.77 us (2%)
  between operations  0.7 us (2%)
    pallas_call x1, Pallas kernels, shards(): pl.pallas_call(kernel, out_shape=[jax.ShapeDtypeStruct((121, 512), F32),...  37.3 us
    unnamed x16, local copies, waits for them, and re-layouts  4.93 us

profile of v1, /device:TPU:1, one launch (start us, length us, event | category | flops | bytes accessed | tf_op | source)
XLA Modules:
  0.0 43.7 jit_solution(11875582280163100706)
XLA Ops:
  0.6 0.0 copy-start.3
  0.6 0.0 copy-start.4
  0.7 0.0 copy-start.6
  0.7 0.8 %multiply_add_fusion.index_ref = s32[1,4096]{1,0:T(1,128)S(1)} fusion(s32[1,4096]{1,0:T(1,128)} %param.15, s32[1,4096]{1,0:T(1,128)} %param.17), kind=kLoop, calls=%fused_computation | loop fusion | flops 8192 | bytes 49152 | tf_op jit(solution)/shard_map/add | solution.py:341
  1.4 0.0 copy-done.3
  1.4 0.0 copy-done.4
  1.5 0.0 copy-done.6
  1.5 0.0 copy-start
  1.5 1.0 %copy-done = f32[8,121,121]{2,0,1:T(8,128)S(1)} copy-done((f32[8,121,121]{2,0,1:T(8,128)S(1)}, f32[8,121,121]{2,0,1:T(8,128)}, u32[]{:S(2)}) %copy-start) | copy-done | bytes 468536
  2.5 0.0 copy-start.1
  2.5 0.9 %copy-done.1 = f32[121,512]{1,0:T(8,128)S(1)} copy-done((f32[121,512]{1,0:T(8,128)S(1)}, f32[121,512]{1,0:T(8,128)}, u32[]{:S(2)}) %copy-start.1) | copy-done | bytes 247832
  3.5 0.0 copy-start.2
  3.5 0.9 %copy-done.2 = f32[3,8192]{1,0:T(4,128)S(1)} copy-done((f32[3,8192]{1,0:T(4,128)S(1)}, f32[3,8192]{1,0:T(4,128)}, u32[]{:S(2)}) %copy-start.2) | copy-done | bytes 98328
  4.4 0.0 copy-start.5
  4.4 0.7 %copy-done.5 = s32[1,4096]{1,0:T(1,128)S(1)} copy-done((s32[1,4096]{1,0:T(1,128)S(1)}, s32[1,4096]{1,0:T(1,128)}, u32[]{:S(2)}) %copy-start.5) | copy-done | bytes 16408
  5.1 37.3 %shard_map.104 = (f32[121,512]{1,0:T(8,128)S(1)}, f32[64,128]{1,0:T(8,128)S(1)}) custom-call(s32[1,4096]{1,0:T(1,128)S(1)} %multiply_add_fusion.index_ref, f32[3,8192]{1,0:T(4,128)S(1)} %copy-done.2, f32[64,128]{1,0:T(8,128)S(1)} %bitcast.6, f32[121,512]{1,0:T(8,128)S(1)} %copy-done.1, f32[121,8,121]{2,1,0:T(8,128)S(1)} %bitcast.4, s32[1,1024]{1,0:T(1,128)S(1)} %copy-done.6, ...), custom_call_target="tpu_custom_call" | custom-call | tf_op jit(solution)/shard_map/pallas_call | solution.py:343
  42.4 0.7 %copy.13 = f32[121,512]{1,0:T(8,128)} copy(f32[121,512]{1,0:T(8,128)S(1)} %get-tuple-element.8) | data formatting | bytes 495616
  43.1 0.6 %copy.14 = f32[8192]{0:T(1024)} copy(f32[8192]{0:T(1024)S(1)} %bitcast.5) | data formatting | bytes 65536
Async XLA Ops:
  0.6 0.8 %copy-start.3 = (f32[8192]{0:T(1024)S(1)}, f32[8192]{0:T(1024)}, u32[]{:S(2)}) copy-start(f32[8192]{0:T(1024)} %param.10) | copy-start | bytes 98308
  0.6 0.8 %copy-start.4 = (s32[512,8]{0,1:T(8,128)S(1)}, s32[512,8]{0,1:T(8,128)}, u32[]{:S(2)}) copy-start(s32[512,8]{0,1:T(8,128)} %param.14) | copy-start | bytes 49156
  0.7 0.8 %copy-start.6 = (s32[1,1024]{1,0:T(1,128)S(1)}, s32[1,1024]{1,0:T(1,128)}, u32[]{:S(2)}) copy-start(s32[1,1024]{1,0:T(1,128)} %send_ref.1) | copy-start | bytes 12292
  1.5 1.0 %copy-start = (f32[8,121,121]{2,0,1:T(8,128)S(1)}, f32[8,121,121]{2,0,1:T(8,128)}, u32[]{:S(2)}) copy-start(f32[8,121,121]{2,0,1:T(8,128)} %param.12) | copy-start | bytes 1405540
  2.5 0.9 %copy-start.1 = (f32[121,512]{1,0:T(8,128)S(1)}, f32[121,512]{1,0:T(8,128)}, u32[]{:S(2)}) copy-start(f32[121,512]{1,0:T(8,128)} %mult_ref.1) | copy-start | bytes 743428
  3.5 0.9 %copy-start.2 = (f32[3,8192]{1,0:T(4,128)S(1)}, f32[3,8192]{1,0:T(4,128)}, u32[]{:S(2)}) copy-start(f32[3,8192]{1,0:T(4,128)} %coords_ref.1) | copy-start | bytes 294916
  4.4 0.7 %copy-start.5 = (s32[1,4096]{1,0:T(1,128)S(1)}, s32[1,4096]{1,0:T(1,128)}, u32[]{:S(2)}) copy-start(s32[1,4096]{1,0:T(1,128)} %target_ref.1) | copy-start | bytes 49156

commit v2 on v1

--- a/solution.py
+++ b/solution.py
@@ -57,21 +57,39 @@
         lane_ref[j] = (leaf & 1) * 64 + (leaf >> 3)
 
 
-def near_gather(window, tile_ref, lane_ref, sources):
+def near_hot(lane_ref, hots):
+    spots = lax.broadcasted_iota(I32, (128, 128), 0)
+    for step in range(16):
+        j, n = step // 4, 2 * (step % 4)
+        for u in range(2):
+            hit = (spots == lane_ref[j, n + u : n + u + 1, :]).astype(BF16)
+            hots[step, 0:128, 128 * u : 128 * u + 128] = hit
+            hots[step, 128:256, 128 * u : 128 * u + 128] = hit
+
+
+def near_table(window, cells, block):
+    rows = slice(256 * block, 256 * block + 256)
+    high, low = split(window[4 * block : 4 * block + 4].reshape(256, 128))
+    cells[rows, 0:128] = high
+    cells[rows, 128:256] = low
+
+
+def near_gather(cells, tile_ref, hots, sources):
     def body(step, carry):
-        j, n = step // 8, step % 8
-        tile = jnp.broadcast_to(tile_ref[j, pl.ds(n, 1), :], (8, 128))
-        spot = jnp.broadcast_to(lane_ref[j, pl.ds(n, 1), :], (8, 128))
-        masks = [tile == k for k in range(12)]
-        for r in range(8):
-            rows = slice(8 * r, 8 * r + 8)
-            got = take(window[0, rows, :], spot)
-            for k in range(1, 12):
-                got = jnp.where(masks[k], take(window[k, rows, :], spot), got)
-            sources[j, n, rows, :] = got
+        j, n = step // 4, 2 * (step % 4)
+        got = jnp.dot(cells[...], hots[step], preferred_element_type=F32)
+        for u in range(2):
+            tile = jnp.broadcast_to(tile_ref[j, pl.ds(n + u, 1), :], (8, 128))
+            masks = [tile == k for k in range(1, 12)]
+            cols = slice(128 * u, 128 * u + 128)
+            for row in range(0, 64, 8):
+                value = got[row : row + 8, cols]
+                for k in range(1, 12):
+                    value = jnp.where(masks[k - 1], got[64 * k + row : 64 * k + row + 8, cols], value)
+                sources[j, n + u, row : row + 8, :] = value
         return carry
 
-    lax.fori_loop(0, 32, body, 0)
+    lax.fori_loop(0, 16, body, 0)
 
 
 def near_sum(own, sources, pot):
@@ -133,23 +151,34 @@
         hot[:, cols] = (lax.broadcasted_iota(I32, (512, 256), 0) == target_ref[:, cols]).astype(BF16)
 
 
-def collect(index_ref, table, picked):
+def collect_sum(index_ref, table, hot, even, odd, total, size):
+    chunks = 4096 // size
+
+    def collect(base, picked):
+        for u in range(size):
+            picked[u : u + 1, :] = table[pl.ds(index_ref[0, base + u], 1), :]
+
+    def add(base, picked):
+        high, low = split(picked[...])
+        both = jnp.concatenate([high, low], axis=1)
+        cols = pl.ds(pl.multiple_of(base, size), size)
+        total[...] += jnp.dot(hot[:, cols], both, preferred_element_type=F32)
+
+    total[...] = jnp.zeros_like(total)
+    collect(0, even)
+
     def body(step, carry):
-        base = step * 64
-        for u in range(64):
-            picked[pl.ds(base + u, 1), :] = table[pl.ds(index_ref[0, base + u], 1), :]
+        base = step * (2 * size)
+        collect(base + size, odd)
+        add(base, even)
+        collect(base + 2 * size, even)
+        add(base + size, odd)
         return carry
 
-    lax.fori_loop(0, 64, body, 0)
-
-
-def gather_sum(hot, picked, total):
-    total[...] = jnp.zeros_like(total)
-    for k in range(8):
-        rows = slice(512 * k, 512 * k + 512)
-        high, low = split(picked[rows, :])
-        both = jnp.concatenate([high, low], axis=1)
-        total[...] += jnp.dot(hot[:, rows], both, preferred_element_type=F32)
+    lax.fori_loop(0, chunks // 2 - 1, body, 0)
+    collect(4096 - size, odd)
+    add(4096 - 2 * size, even)
+    add(4096 - size, odd)
 
 
 def far_out(total, out_ref):
@@ -159,23 +188,58 @@
 
 
 MESH = pl.DeviceIdType.MESH
+GROUPS = 64
+
+
+def each_other(g, act):
+    x, y, c = g // 16, (g // 2) % 8, g % 2
+
+    def body(step, carry):
+        i, r = step // 8, step % 8
+        turn = (i + 1) // 2
+        dy = jnp.where(i % 2 == 1, 4 - turn, 4 + turn)
+        other = lax.rem(x + r // 2, 4) * 16 + lax.rem(y + dy, 8) * 2 + lax.rem(c + r % 2, 2)
+
+        @pl.when((other != g) & (other != 0))
+        def _():
+            act(other)
+
+        return carry
+
+    lax.fori_loop(0, GROUPS, body, 0)
 
 
 def kernel(
-    index_ref,
-    coords_ref,
-    charges_ref,
-    mult_ref,
-    ops_ref,
-    send_ref,
-    near_ref,
-    target_ref,
-    far_ref,
-    pot_ref,
+    coords_hbm,
+    charges_hbm,
+    mult_hbm,
+    ops_hbm,
+    send_hbm,
+    near_hbm,
+    source_hbm,
+    target_hbm,
+    kind_hbm,
+    far_hbm,
+    pot_hbm,
+    coords,
+    charges,
+    mult,
+    ops,
+    sends,
+    near,
+    entry_source,
+    entry_target,
+    entry_kind,
+    index_row,
+    index,
+    far_out_rows,
+    pot_out_rows,
     stage,
     window,
     tile,
     spot,
+    hots,
+    cells,
     sources,
     pot,
     flip,
@@ -187,24 +251,41 @@
     second,
     table,
     hot,
-    picked,
+    even,
+    odd,
     total,
+    load_sem,
+    store_sem,
     halo_send,
     halo_recv,
     rows_send,
     rows_recv,
 ):
-    slabs, groups = lax.axis_size("slab"), lax.axis_size("grp")
+    slabs = lax.axis_size("slab")
     s, g = lax.axis_index("slab"), lax.axis_index("grp")
-
     barrier = pltpu.get_barrier_semaphore()
 
-    def greet(d, carry):
-        other = lax.rem(g + d, groups)
+    def greet(other):
         pl.semaphore_signal(barrier, inc=1, device_id={"grp": other}, device_id_type=MESH)
-        return carry
-
-    lax.fori_loop(1, groups, greet, 0)
+
+    loads = [
+        pltpu.make_async_copy(source, target, load_sem.at[i])
+        for i, (source, target) in enumerate(
+            [
+                (mult_hbm, mult),
+                (send_hbm, sends),
+                (coords_hbm, coords),
+                (charges_hbm, charges),
+                (near_hbm, near),
+                (ops_hbm, ops),
+                (source_hbm, entry_source),
+                (kind_hbm, entry_kind),
+                (target_hbm, entry_target),
+            ]
+        )
+    ]
+    for load in loads:
+        load.start()
 
     @pl.when(s > 0)
     def _():
@@ -214,22 +295,24 @@
     def _():
         pl.semaphore_signal(barrier, inc=1, device_id={"slab": s + 1}, device_id_type=MESH)
 
-    send_rows(mult_ref, send_ref, held, outgoing)
+    @pl.when(g != 0)
+    def _():
+        each_other(g, greet)
+
+    loads[0].wait()
+    loads[1].wait()
+    send_rows(mult, sends, held, outgoing)
+    loads[2].wait()
+    loads[3].wait()
     own = window.at[4:8]
-    own_window(coords_ref, charges_ref, stage, own)
+    own_window(coords, charges, stage, own)
 
     inner = jnp.where(s > 0, 1, 0) + jnp.where(s < slabs - 1, 1, 0)
-    pl.semaphore_wait(barrier, groups - 1 + inner)
-
-    def rows_copy(other):
-        return pltpu.make_async_remote_copy(
-            src_ref=outgoing.at[pl.ds(pl.multiple_of(16 * other, 16), 16)],
-            dst_ref=received.at[pl.ds(pl.multiple_of(16 * g, 16), 16)],
-            send_sem=rows_send,
-            recv_sem=rows_recv.at[g // 8],
-            device_id={"grp": other},
-            device_id_type=MESH,
-        )
+    pl.semaphore_wait(barrier, GROUPS - 1 - jnp.where(g != 0, 1, 0) + inner)
+
+    @pl.when(g != 0)
+    def _():
+        greet(0)
 
     up = pltpu.make_async_remote_copy(
         src_ref=own,
@@ -256,18 +339,42 @@
     def _():
         down.start()
 
-    def send(d, carry):
-        rows_copy(lax.rem(g + d, groups)).start()
-        return carry
-
-    lax.fori_loop(1, groups, send, 0)
+    @pl.when((g == 0) & (s > 0))
+    def _():
+        each_other(g, greet)
+
+    def rows_copy(other):
+        return pltpu.make_async_remote_copy(
+            src_ref=outgoing.at[pl.ds(pl.multiple_of(16 * other, 16), 16)],
+            dst_ref=received.at[pl.ds(pl.multiple_of(16 * g, 16), 16)],
+            send_sem=rows_send,
+            recv_sem=rows_recv.at[g // 16],
+            device_id={"grp": other},
+            device_id_type=MESH,
+        )
+
+    each_other(g, lambda other: rows_copy(other).start())
+
+    @pl.when((g == 0) & (s == 0))
+    def _():
+        each_other(g, greet)
 
     mine = pl.ds(pl.multiple_of(16 * g, 16), 16)
     received[mine, :] = outgoing[mine, :]
 
-    near_index(near_ref, tile, spot)
-    operator_parts(ops_ref, pad, first, second)
-    target_table(target_ref, hot)
+    loads[4].wait()
+    near_index(near, tile, spot)
+    near_hot(spot, hots)
+    loads[5].wait()
+    operator_parts(ops, pad, first, second)
+    loads[6].wait()
+    loads[7].wait()
+    index_row[...] = entry_kind[...] * 1024 + entry_source[...]
+    index_load = pltpu.make_async_copy(index_row, index, load_sem.at[9])
+    index_load.start()
+    loads[8].wait()
+    target_table(entry_target, hot)
+    near_table(window, cells, 1)
 
     @pl.when(s == 0)
     def _():
@@ -285,9 +392,20 @@
     def _():
         down.wait_recv()
 
-    near_gather(window, tile, spot, sources)
+    near_table(window, cells, 0)
+    near_table(window, cells, 2)
+    near_gather(cells, tile, hots, sources)
+
+    @pl.when(g != 0)
+    def _():
+        pl.semaphore_wait(barrier, 1)
+        rows_copy(0).start()
+
     near_sum(own, sources, pot)
-    near_out(pot, flip, pot_ref)
+    near_out(pot, flip, pot_out_rows)
+    pot_store = pltpu.make_async_copy(pot_out_rows, pot_hbm, store_sem.at[0])
+    pot_store.start()
+    index_load.wait()
 
     def arrived(count, k):
         block = pl.ds(0, 16 * count)
@@ -296,27 +414,22 @@
             dst_ref=received.at[block],
             send_sem=rows_send,
             recv_sem=rows_recv.at[k],
-            device_id={"grp": lax.rem(g + 1, groups)},
+            device_id={"grp": lax.rem(g + 1, GROUPS)},
             device_id_type=MESH,
         )
 
-    for k in range(groups // 8):
-
-        @pl.when(g // 8 == k)
-        def _():
-            arrived(7, k).wait_recv()
-
-        @pl.when(g // 8 != k)
-        def _():
-            arrived(8, k).wait_recv()
-
-        translate(received[128 * k : 128 * k + 128, :], first, second, table, 128 * k)
-
-    collect(index_ref, table, picked)
-    gather_sum(hot, picked, total)
-    far_out(total, far_ref)
-
-    arrived(groups - 1, 0).wait_send()
+    for turn in (0, 1, 3, 2):
+        k = lax.rem(g // 16 + turn, 4)
+        arrived(15 if turn == 0 else 16, k).wait_recv()
+        start = pl.multiple_of(256 * k, 256)
+        translate(received[pl.ds(start, 256), :], first, second, table, start)
+
+    collect_sum(index, table, hot, even, odd, total, 512)
+    far_out(total, far_out_rows)
+    far_store = pltpu.make_async_copy(far_out_rows, far_hbm, store_sem.at[1])
+    far_store.start()
+
+    arrived(GROUPS - 1, 0).wait_send()
 
     @pl.when(s < slabs - 1)
     def _():
@@ -325,6 +438,9 @@
     @pl.when(s > 0)
     def _():
         down.wait_send()
+
+    pot_store.wait()
+    far_store.wait()
 
 
 def shards(
@@ -338,48 +454,67 @@
     m2l_target,
     m2l_operator,
 ):
-    index = m2l_operator * 1024 + m2l_source
-    vmem = pl.BlockSpec(memory_space=pltpu.VMEM)
+    hbm = pl.BlockSpec(memory_space=pltpu.HBM)
+    vmem, dma = pltpu.VMEM, pltpu.SemaphoreType.DMA
     far, pot = pl.pallas_call(
         kernel,
         out_shape=[jax.ShapeDtypeStruct((121, 512), F32), jax.ShapeDtypeStruct((64, 128), F32)],
-        in_specs=[pl.BlockSpec(memory_space=pltpu.SMEM)] + [vmem] * 7,
-        out_specs=[vmem, vmem],
+        in_specs=[hbm] * 9,
+        out_specs=[hbm] * 2,
         scratch_shapes=[
-            pltpu.VMEM((2, 128, 128), F32),
-            pltpu.VMEM((12, 64, 128), F32),
-            pltpu.VMEM((4, 8, 128), I32),
-            pltpu.VMEM((4, 8, 128), I32),
-            pltpu.VMEM((4, 8, 64, 128), F32),
-            pltpu.VMEM((4, 16, 128), F32),
-            pltpu.VMEM((128, 128), F32),
-            pltpu.VMEM((128, 512), F32),
-            pltpu.VMEM((1024, 128), F32),
-            pltpu.VMEM((1024, 128), F32),
-            pltpu.VMEM((128, 128), F32),
-            pltpu.VMEM((4, 256, 256), BF16),
-            pltpu.VMEM((4, 256, 128), BF16),
-            pltpu.VMEM((8192, 128), F32),
-            pltpu.VMEM((512, 4096), BF16),
-            pltpu.VMEM((4096, 128), F32),
-            pltpu.VMEM((512, 256), F32),
-            pltpu.SemaphoreType.DMA((2,)),
-            pltpu.SemaphoreType.DMA((2,)),
-            pltpu.SemaphoreType.DMA,
-            pltpu.SemaphoreType.DMA((8,)),
+            vmem((3, 8192), F32),
+            vmem((64, 128), F32),
+            vmem((121, 512), F32),
+            vmem((121, 8, 121), F32),
+            vmem((1, 1024), I32),
+            vmem((8, 512), I32),
+            vmem((1, 4096), I32),
+            vmem((1, 4096), I32),
+            vmem((1, 4096), I32),
+            vmem((1, 4096), I32),
+            pltpu.SMEM((1, 4096), I32),
+            vmem((121, 512), F32),
+            vmem((64, 128), F32),
+            vmem((2, 128, 128), F32),
+            vmem((12, 64, 128), F32),
+            vmem((4, 8, 128), I32),
+            vmem((4, 8, 128), I32),
+            vmem((16, 256, 256), BF16),
+            vmem((768, 256), BF16),
+            vmem((4, 8, 64, 128), F32),
+            vmem((4, 16, 128), F32),
+            vmem((128, 128), F32),
+            vmem((128, 512), F32),
+            vmem((1024, 128), F32),
+            vmem((1024, 128), F32),
+            vmem((128, 128), F32),
+            vmem((4, 256, 256), BF16),
+            vmem((4, 256, 128), BF16),
+            vmem((8192, 128), F32),
+            vmem((512, 4096), BF16),
+            vmem((512, 128), F32),
+            vmem((512, 128), F32),
+            vmem((512, 256), F32),
+            dma((10,)),
+            dma((2,)),
+            dma((2,)),
+            dma((2,)),
+            dma,
+            dma((4,)),
         ],
         compiler_params=pltpu.CompilerParams(
-            collective_id=0, has_side_effects=True, vmem_limit_bytes=40 * 2**20
+            collective_id=0, has_side_effects=True, vmem_limit_bytes=60 * 2**20
         ),
     )(
-        index,
         coords,
         charges.reshape(64, 128),
         multipoles,
         jnp.transpose(operators, (1, 0, 2)),
         send_list,
         near_list.T,
+        m2l_source,
         m2l_target,
+        m2l_operator,
     )
     return far, pot.reshape(-1)
 

time: 44.1 us -> 36.5 us (0.83)
  the two profiles are of different devices: /device:TPU:1 before, /device:TPU:192 now
where the time goes in v2:
time: 36.5 us; the launch traced here: 36.3 us
  Pallas kernels  33.4 us (92%)
  local copies, waits for them, and re-layouts  2.3 us (6%)
  between operations  0.65 us (2%)
    pallas_call x1, Pallas kernels, shards(): pl.pallas_call(kernel, out_shape=[jax.ShapeDtypeStruct((121, 512), F32),...  33.4 us
    unnamed x4, local copies, waits for them, and re-layouts  2.3 us

profile of v2, /device:TPU:192, one launch (start us, length us, event | category | flops | bytes accessed | tf_op | source)
XLA Modules:
  0.0 36.3 jit_solution(11698142136240378320)
XLA Ops:
  0.6 33.4 %shard_map.104 = (f32[121,512]{1,0:T(8,128)}, f32[64,128]{1,0:T(8,128)}) custom-call(f32[3,8192]{1,0:T(4,128)} %coords_hbm.1, f32[64,128]{1,0:T(8,128)} %bitcast.5, f32[121,512]{1,0:T(8,128)} %mult_hbm.1, f32[121,8,121]{2,1,0:T(8,128)} %bitcast.4, s32[1,1024]{1,0:T(1,128)} %send_hbm.1, s32[8,512]{1,0:T(8,128)} %bitcast.7, s32[1,4096]{1,0:T(1,128)} %source_hbm.1, ...), custom_call_target="tpu_custom_call" | custom-call | tf_op jit(solution)/shard_map/pallas_call | solution.py:459
  34.0 0.0 copy-start
  34.0 1.7 %copy.13 = f32[121,512]{1,0:T(8,128)} copy(f32[121,512]{1,0:T(8,128)} %get-tuple-element.8) | data formatting | bytes 495616
  35.7 0.0 copy-done
  35.7 0.6 %copy.14 = f32[8192]{0:T(1024)} copy(f32[8192]{0:T(1024)S(1)} %bitcast.6) | data formatting | bytes 65536
Async XLA Ops:
  34.0 1.7 %copy-start = (f32[64,128]{1,0:T(8,128)S(1)}, f32[64,128]{1,0:T(8,128)}, u32[]{:S(2)}) copy-start(f32[64,128]{1,0:T(8,128)} %get-tuple-element.5) | copy-start | bytes 98308

commit v3 on v2

--- a/solution.py
+++ b/solution.py
@@ -191,7 +191,7 @@
 GROUPS = 64
 
 
-def each_other(g, act):
+def each_other(g, skip, act):
     x, y, c = g // 16, (g // 2) % 8, g % 2
 
     def body(step, carry):
@@ -200,7 +200,7 @@
         dy = jnp.where(i % 2 == 1, 4 - turn, 4 + turn)
         other = lax.rem(x + r // 2, 4) * 16 + lax.rem(y + dy, 8) * 2 + lax.rem(c + r % 2, 2)
 
-        @pl.when((other != g) & (other != 0))
+        @pl.when((other != g) & (other != skip))
         def _():
             act(other)
 
@@ -219,8 +219,8 @@
     source_hbm,
     target_hbm,
     kind_hbm,
-    far_hbm,
-    pot_hbm,
+    far_rows,
+    pot_rows,
     coords,
     charges,
     mult,
@@ -232,8 +232,6 @@
     entry_kind,
     index_row,
     index,
-    far_out_rows,
-    pot_out_rows,
     stage,
     window,
     tile,
@@ -255,7 +253,6 @@
     odd,
     total,
     load_sem,
-    store_sem,
     halo_send,
     halo_recv,
     rows_send,
@@ -295,9 +292,13 @@
     def _():
         pl.semaphore_signal(barrier, inc=1, device_id={"slab": s + 1}, device_id_type=MESH)
 
-    @pl.when(g != 0)
-    def _():
-        each_other(g, greet)
+    late = (s == 0) & (g == 0)
+    meets_late = (s == 0) & (g != 0)
+    skip = jnp.where(s == 0, 0, GROUPS)
+
+    @pl.when(jnp.logical_not(late))
+    def _():
+        each_other(g, skip, greet)
 
     loads[0].wait()
     loads[1].wait()
@@ -308,9 +309,9 @@
     own_window(coords, charges, stage, own)
 
     inner = jnp.where(s > 0, 1, 0) + jnp.where(s < slabs - 1, 1, 0)
-    pl.semaphore_wait(barrier, GROUPS - 1 - jnp.where(g != 0, 1, 0) + inner)
-
-    @pl.when(g != 0)
+    pl.semaphore_wait(barrier, GROUPS - 1 - jnp.where(meets_late, 1, 0) + inner)
+
+    @pl.when(meets_late)
     def _():
         greet(0)
 
@@ -339,10 +340,6 @@
     def _():
         down.start()
 
-    @pl.when((g == 0) & (s > 0))
-    def _():
-        each_other(g, greet)
-
     def rows_copy(other):
         return pltpu.make_async_remote_copy(
             src_ref=outgoing.at[pl.ds(pl.multiple_of(16 * other, 16), 16)],
@@ -353,11 +350,11 @@
             device_id_type=MESH,
         )
 
-    each_other(g, lambda other: rows_copy(other).start())
-
-    @pl.when((g == 0) & (s == 0))
-    def _():
-        each_other(g, greet)
+    each_other(g, skip, lambda other: rows_copy(other).start())
+
+    @pl.when(late)
+    def _():
+        each_other(g, skip, greet)
 
     mine = pl.ds(pl.multiple_of(16 * g, 16), 16)
     received[mine, :] = outgoing[mine, :]
@@ -396,15 +393,8 @@
     near_table(window, cells, 2)
     near_gather(cells, tile, hots, sources)
 
-    @pl.when(g != 0)
-    def _():
-        pl.semaphore_wait(barrier, 1)
-        rows_copy(0).start()
-
     near_sum(own, sources, pot)
-    near_out(pot, flip, pot_out_rows)
-    pot_store = pltpu.make_async_copy(pot_out_rows, pot_hbm, store_sem.at[0])
-    pot_store.start()
+    near_out(pot, flip, pot_rows)
     index_load.wait()
 
     def arrived(count, k):
@@ -418,16 +408,26 @@
             device_id_type=MESH,
         )
 
-    for turn in (0, 1, 3, 2):
-        k = lax.rem(g // 16 + turn, 4)
-        arrived(15 if turn == 0 else 16, k).wait_recv()
-        start = pl.multiple_of(256 * k, 256)
-        translate(received[pl.ds(start, 256), :], first, second, table, start)
+    for k in (1, 2, 3, 0):
+        if k == 0:
+
+            @pl.when(meets_late)
+            def _():
+                pl.semaphore_wait(barrier, 1)
+                rows_copy(0).start()
+
+        @pl.when(g // 16 == k)
+        def _():
+            arrived(15, k).wait_recv()
+
+        @pl.when(g // 16 != k)
+        def _():
+            arrived(16, k).wait_recv()
+
+        translate(received[256 * k : 256 * k + 256, :], first, second, table, 256 * k)
 
     collect_sum(index, table, hot, even, odd, total, 512)
-    far_out(total, far_out_rows)
-    far_store = pltpu.make_async_copy(far_out_rows, far_hbm, store_sem.at[1])
-    far_store.start()
+    far_out(total, far_rows)
 
     arrived(GROUPS - 1, 0).wait_send()
 
@@ -438,9 +438,6 @@
     @pl.when(s > 0)
     def _():
         down.wait_send()
-
-    pot_store.wait()
-    far_store.wait()
 
 
 def shards(
@@ -454,13 +451,24 @@
     m2l_target,
     m2l_operator,
 ):
+    operands = (
+        coords,
+        charges.reshape(64, 128),
+        multipoles,
+        jnp.transpose(operators, (1, 0, 2)),
+        send_list,
+        near_list.T,
+        m2l_source,
+        m2l_target,
+        m2l_operator,
+    )
     hbm = pl.BlockSpec(memory_space=pltpu.HBM)
     vmem, dma = pltpu.VMEM, pltpu.SemaphoreType.DMA
     far, pot = pl.pallas_call(
         kernel,
-        out_shape=[jax.ShapeDtypeStruct((121, 512), F32), jax.ShapeDtypeStruct((64, 128), F32)],
+        out_shape=[vmem((121, 512), F32), vmem((64, 128), F32)],
         in_specs=[hbm] * 9,
-        out_specs=[hbm] * 2,
+        out_specs=[pl.BlockSpec(memory_space=vmem)] * 2,
         scratch_shapes=[
             vmem((3, 8192), F32),
             vmem((64, 128), F32),
@@ -473,8 +481,6 @@
             vmem((1, 4096), I32),
             vmem((1, 4096), I32),
             pltpu.SMEM((1, 4096), I32),
-            vmem((121, 512), F32),
-            vmem((64, 128), F32),
             vmem((2, 128, 128), F32),
             vmem((12, 64, 128), F32),
             vmem((4, 8, 128), I32),
@@ -498,24 +504,13 @@
             dma((10,)),
             dma((2,)),
             dma((2,)),
-            dma((2,)),
             dma,
             dma((4,)),
         ],
         compiler_params=pltpu.CompilerParams(
-            collective_id=0, has_side_effects=True, vmem_limit_bytes=60 * 2**20
+            collective_id=0, has_side_effects=True, vmem_limit_bytes=48 * 2**20
         ),
-    )(
-        coords,
-        charges.reshape(64, 128),
-        multipoles,
-        jnp.transpose(operators, (1, 0, 2)),
-        send_list,
-        near_list.T,
-        m2l_source,
-        m2l_target,
-        m2l_operator,
-    )
+    )(*(pltpu.with_memory_space_constraint(x, pltpu.HBM) for x in operands))
     return far, pot.reshape(-1)
 
 

time: 36.5 us -> 32.1 us (0.88)
  Pallas kernels: 33.4 us -> 30 us
  local copies, waits for them, and re-layouts: 2.3 us -> 1.32 us
    pallas_call x1, Pallas kernels: 33.4 us -> 30 us  [shards(): pl.pallas_call(kernel, out_shape=[vmem((121, 512), F32), vmem((64, 128),...]
    unnamed x4 -> x2, local copies, waits for them, and re-layouts: 2.3 us -> 1.32 us
where the time goes in v3:
time: 32.1 us; the launch traced here: 31.9 us
  Pallas kernels  30 us (93%)
  local copies, waits for them, and re-layouts  1.32 us (4%)
  between operations  0.64 us (2%)
    pallas_call x1, Pallas kernels, shards(): pl.pallas_call(kernel, out_shape=[vmem((121, 512), F32), vmem((64, 128),...  30 us
    unnamed x2, local copies, waits for them, and re-layouts  1.32 us

profile of v3, /device:TPU:192, one launch (start us, length us, event | category | flops | bytes accessed | tf_op | source)
XLA Modules:
  0.0 31.9 jit_solution(13047003564315479442)
XLA Ops:
  0.6 30.0 %shard_map.104 = (f32[121,512]{1,0:T(8,128)S(1)}, f32[64,128]{1,0:T(8,128)S(1)}) custom-call(f32[3,8192]{1,0:T(4,128)} %coords_hbm.1, f32[64,128]{1,0:T(8,128)} %bitcast.6, f32[121,512]{1,0:T(8,128)} %mult_hbm.1, f32[121,8,121]{2,1,0:T(8,128)} %bitcast.5, s32[1,1024]{1,0:T(1,128)} %send_hbm.1, s32[8,512]{1,0:T(8,128)} %bitcast.7, s32[1,4096]{1,0:T(1,128)} %source_hbm.1, ...), custom_call_target="tpu_custom_call" | custom-call | tf_op jit(solution)/shard_map/pallas_call | solution.py:467
  30.6 0.7 %copy.13 = f32[121,512]{1,0:T(8,128)} copy(f32[121,512]{1,0:T(8,128)S(1)} %get-tuple-element.6) | data formatting | bytes 495616
  31.3 0.6 %copy.14 = f32[8192]{0:T(1024)} copy(f32[8192]{0:T(1024)S(1)} %bitcast.4) | data formatting | bytes 65536

commit v4 on v3

--- a/solution.py
+++ b/solution.py
@@ -1,3 +1,4 @@
+import functools
 import jax
 import jax.numpy as jnp
 from jax import lax
@@ -192,21 +193,18 @@
 
 
 def each_other(g, skip, act):
-    x, y, c = g // 16, (g // 2) % 8, g % 2
-
-    def body(step, carry):
-        i, r = step // 8, step % 8
-        turn = (i + 1) // 2
-        dy = jnp.where(i % 2 == 1, 4 - turn, 4 + turn)
-        other = lax.rem(x + r // 2, 4) * 16 + lax.rem(y + dy, 8) * 2 + lax.rem(c + r % 2, 2)
-
-        @pl.when((other != g) & (other != skip))
-        def _():
-            act(other)
-
-        return carry
-
-    lax.fori_loop(0, GROUPS, body, 0)
+    columns = [lax.rem(g // 16 + d, 4) * 16 for d in range(4)]
+    rows = [lax.rem((g // 2) % 8 + d, 8) * 2 for d in range(8)]
+    cores = [g % 2, 1 - g % 2]
+    for dy in (4, 3, 5, 2, 6, 1, 7, 0):
+        for dx in (2, 1, 3, 0):
+            for dc in (0, 1):
+                if (dx, dy, dc) != (0, 0, 0):
+                    other = columns[dx] + rows[dy] + cores[dc]
+                    if skip is None:
+                        act(other)
+                    else:
+                        pl.when(other != skip)(functools.partial(act, other))
 
 
 def kernel(
@@ -294,11 +292,17 @@
 
     late = (s == 0) & (g == 0)
     meets_late = (s == 0) & (g != 0)
-    skip = jnp.where(s == 0, 0, GROUPS)
-
-    @pl.when(jnp.logical_not(late))
-    def _():
-        each_other(g, skip, greet)
+
+    def each(act):
+        @pl.when(s == 0)
+        def _():
+            each_other(g, 0, act)
+
+        @pl.when(s != 0)
+        def _():
+            each_other(g, None, act)
+
+    pl.when(jnp.logical_not(late))(functools.partial(each, greet))
 
     loads[0].wait()
     loads[1].wait()
@@ -340,24 +344,26 @@
     def _():
         down.start()
 
+    y = (g // 2) % 8
+    mine = pl.ds(pl.multiple_of(y * 128 + (g // 16) * 32 + (g % 2) * 16, 16), 16)
+
     def rows_copy(other):
         return pltpu.make_async_remote_copy(
             src_ref=outgoing.at[pl.ds(pl.multiple_of(16 * other, 16), 16)],
-            dst_ref=received.at[pl.ds(pl.multiple_of(16 * g, 16), 16)],
+            dst_ref=received.at[mine],
             send_sem=rows_send,
-            recv_sem=rows_recv.at[g // 16],
+            recv_sem=rows_recv.at[y // 2],
             device_id={"grp": other},
             device_id_type=MESH,
         )
 
-    each_other(g, skip, lambda other: rows_copy(other).start())
+    each(lambda other: rows_copy(other).start())
 
     @pl.when(late)
     def _():
-        each_other(g, skip, greet)
-
-    mine = pl.ds(pl.multiple_of(16 * g, 16), 16)
-    received[mine, :] = outgoing[mine, :]
+        each_other(g, None, greet)
+
+    received[mine, :] = outgoing[pl.ds(pl.multiple_of(16 * g, 16), 16), :]
 
     loads[4].wait()
     near_index(near, tile, spot)
@@ -366,7 +372,9 @@
     operator_parts(ops, pad, first, second)
     loads[6].wait()
     loads[7].wait()
-    index_row[...] = entry_kind[...] * 1024 + entry_source[...]
+    source = entry_source[...]
+    place = ((source >> 5) & 7) * 128 + (source >> 8) * 32 + (source & 31)
+    index_row[...] = entry_kind[...] * 1024 + place
     index_load = pltpu.make_async_copy(index_row, index, load_sem.at[9])
     index_load.start()
     loads[8].wait()
@@ -408,23 +416,25 @@
             device_id_type=MESH,
         )
 
-    for k in (1, 2, 3, 0):
-        if k == 0:
+    for i, turn in enumerate((2, 1, 3, 0)):
+        k = lax.rem(jnp.where(s == 0, 1 + i, y // 2 + turn), 4)
+        if i == 3:
 
             @pl.when(meets_late)
             def _():
                 pl.semaphore_wait(barrier, 1)
                 rows_copy(0).start()
 
-        @pl.when(g // 16 == k)
+        @pl.when(y // 2 == k)
         def _():
             arrived(15, k).wait_recv()
 
-        @pl.when(g // 16 != k)
+        @pl.when(y // 2 != k)
         def _():
             arrived(16, k).wait_recv()
 
-        translate(received[256 * k : 256 * k + 256, :], first, second, table, 256 * k)
+        start = pl.multiple_of(256 * k, 256)
+        translate(received[pl.ds(start, 256), :], first, second, table, start)
 
     collect_sum(index, table, hot, even, odd, total, 512)
     far_out(total, far_rows)

time: 32.1 us -> 32 us (level)
  no operation moved by 1% of the time
where the time goes in v4:
time: 32 us; the launch traced here: 31.8 us
  Pallas kernels  29.8 us (93%)
  local copies, waits for them, and re-layouts  1.32 us (4%)
  between operations  0.64 us (2%)
    pallas_call x1, Pallas kernels, shards(): pl.pallas_call(kernel, out_shape=[vmem((121, 512), F32), vmem((64, 128),...  29.8 us
    unnamed x2, local copies, waits for them, and re-layouts  1.32 us

profile of v4, /device:TPU:192, one launch (start us, length us, event | category | flops | bytes accessed | tf_op | source)
XLA Modules:
  0.0 31.8 jit_solution(16001613440256120299)
XLA Ops:
  0.6 29.8 %shard_map.104 = (f32[121,512]{1,0:T(8,128)S(1)}, f32[64,128]{1,0:T(8,128)S(1)}) custom-call(f32[3,8192]{1,0:T(4,128)} %coords_hbm.1, f32[64,128]{1,0:T(8,128)} %bitcast.6, f32[121,512]{1,0:T(8,128)} %mult_hbm.1, f32[121,8,121]{2,1,0:T(8,128)} %bitcast.5, s32[1,1024]{1,0:T(1,128)} %send_hbm.1, s32[8,512]{1,0:T(8,128)} %bitcast.7, s32[1,4096]{1,0:T(1,128)} %source_hbm.1, ...), custom_call_target="tpu_custom_call" | custom-call | tf_op jit(solution)/shard_map/pallas_call | solution.py:477
  30.5 0.7 %copy.13 = f32[121,512]{1,0:T(8,128)} copy(f32[121,512]{1,0:T(8,128)S(1)} %get-tuple-element.6) | data formatting | bytes 495616
  31.2 0.6 %copy.14 = f32[8192]{0:T(1024)} copy(f32[8192]{0:T(1024)S(1)} %bitcast.4) | data formatting | bytes 65536

commit v5 on v4

--- a/solution.py
+++ b/solution.py
@@ -192,19 +192,26 @@
 GROUPS = 64
 
 
-def each_other(g, skip, act):
+def each_other(g, skip, act, early=None):
     columns = [lax.rem(g // 16 + d, 4) * 16 for d in range(4)]
     rows = [lax.rem((g // 2) % 8 + d, 8) * 2 for d in range(8)]
     cores = [g % 2, 1 - g % 2]
     for dy in (4, 3, 5, 2, 6, 1, 7, 0):
-        for dx in (2, 1, 3, 0):
-            for dc in (0, 1):
-                if (dx, dy, dc) != (0, 0, 0):
-                    other = columns[dx] + rows[dy] + cores[dc]
-                    if skip is None:
-                        act(other)
-                    else:
-                        pl.when(other != skip)(functools.partial(act, other))
+
+        def row(dy=dy):
+            for dx in (2, 1, 3, 0):
+                for dc in (0, 1):
+                    if (dx, dy, dc) != (0, 0, 0):
+                        other = columns[dx] + rows[dy] + cores[dc]
+                        if skip is None:
+                            act(other)
+                        else:
+                            pl.when(other != skip)(functools.partial(act, other))
+
+        if early is None:
+            row()
+        else:
+            pl.when(rows[dy] < 8 if early else rows[dy] >= 8)(row)
 
 
 def kernel(
@@ -293,14 +300,14 @@
     late = (s == 0) & (g == 0)
     meets_late = (s == 0) & (g != 0)
 
-    def each(act):
+    def each(act, early=None):
         @pl.when(s == 0)
         def _():
-            each_other(g, 0, act)
+            each_other(g, 0, act, early)
 
         @pl.when(s != 0)
         def _():
-            each_other(g, None, act)
+            each_other(g, None, act, early)
 
     pl.when(jnp.logical_not(late))(functools.partial(each, greet))
 
@@ -352,16 +359,13 @@
             src_ref=outgoing.at[pl.ds(pl.multiple_of(16 * other, 16), 16)],
             dst_ref=received.at[mine],
             send_sem=rows_send,
-            recv_sem=rows_recv.at[y // 2],
+            recv_sem=rows_recv.at[jnp.where(late, 4, y // 2)],
             device_id={"grp": other},
             device_id_type=MESH,
         )
 
-    each(lambda other: rows_copy(other).start())
-
-    @pl.when(late)
-    def _():
-        each_other(g, None, greet)
+    each(lambda other: rows_copy(other).start(), True)
+    each(lambda other: rows_copy(other).start(), False)
 
     received[mine, :] = outgoing[pl.ds(pl.multiple_of(16 * g, 16), 16), :]
 
@@ -422,16 +426,17 @@
 
             @pl.when(meets_late)
             def _():
-                pl.semaphore_wait(barrier, 1)
+                arrived(1, 4).wait_recv()
                 rows_copy(0).start()
 
-        @pl.when(y // 2 == k)
-        def _():
-            arrived(15, k).wait_recv()
-
-        @pl.when(y // 2 != k)
-        def _():
-            arrived(16, k).wait_recv()
+        missing = jnp.where(y // 2 == k, 1, 0)
+        if i == 3:
+            missing = missing + jnp.where(meets_late, 1, 0)
+        for count in (14, 15, 16):
+
+            @pl.when(missing == 16 - count)
+            def _():
+                arrived(count, k).wait_recv()
 
         start = pl.multiple_of(256 * k, 256)
         translate(received[pl.ds(start, 256), :], first, second, table, start)
@@ -515,7 +520,7 @@
             dma((2,)),
             dma((2,)),
             dma,
-            dma((4,)),
+            dma((5,)),
         ],
         compiler_params=pltpu.CompilerParams(
             collective_id=0, has_side_effects=True, vmem_limit_bytes=48 * 2**20

time: 32 us -> 32 us (level)
  no operation moved by 1% of the time
where the time goes in v5:
time: 32 us; the launch traced here: 31.8 us
  Pallas kernels  29.9 us (93%)
  local copies, waits for them, and re-layouts  1.32 us (4%)
  between operations  0.64 us (2%)
    pallas_call x1, Pallas kernels, shards(): pl.pallas_call(kernel, out_shape=[vmem((121, 512), F32), vmem((64, 128),...  29.9 us
    unnamed x2, local copies, waits for them, and re-layouts  1.32 us

profile of v5, /device:TPU:192, one launch (start us, length us, event | category | flops | bytes accessed | tf_op | source)
XLA Modules:
  0.0 31.8 jit_solution(11305114498790153825)
XLA Ops:
  0.6 29.9 %shard_map.104 = (f32[121,512]{1,0:T(8,128)S(1)}, f32[64,128]{1,0:T(8,128)S(1)}) custom-call(f32[3,8192]{1,0:T(4,128)} %coords_hbm.1, f32[64,128]{1,0:T(8,128)} %bitcast.6, f32[121,512]{1,0:T(8,128)} %mult_hbm.1, f32[121,8,121]{2,1,0:T(8,128)} %bitcast.5, s32[1,1024]{1,0:T(1,128)} %send_hbm.1, s32[8,512]{1,0:T(8,128)} %bitcast.7, s32[1,4096]{1,0:T(1,128)} %source_hbm.1, ...), custom_call_target="tpu_custom_call" | custom-call | tf_op jit(solution)/shard_map/pallas_call | solution.py:482
  30.5 0.7 %copy.13 = f32[121,512]{1,0:T(8,128)} copy(f32[121,512]{1,0:T(8,128)S(1)} %get-tuple-element.6) | data formatting | bytes 495616
  31.2 0.6 %copy.14 = f32[8192]{0:T(1024)} copy(f32[8192]{0:T(1024)S(1)} %bitcast.4) | data formatting | bytes 65536

commit v6 on v5

--- a/solution.py
+++ b/solution.py
@@ -162,24 +162,15 @@
     def add(base, picked):
         high, low = split(picked[...])
         both = jnp.concatenate([high, low], axis=1)
-        cols = pl.ds(pl.multiple_of(base, size), size)
-        total[...] += jnp.dot(hot[:, cols], both, preferred_element_type=F32)
+        total[...] += jnp.dot(hot[:, base : base + size], both, preferred_element_type=F32)
 
     total[...] = jnp.zeros_like(total)
     collect(0, even)
 
-    def body(step, carry):
-        base = step * (2 * size)
-        collect(base + size, odd)
-        add(base, even)
-        collect(base + 2 * size, even)
-        add(base + size, odd)
-        return carry
-
-    lax.fori_loop(0, chunks // 2 - 1, body, 0)
-    collect(4096 - size, odd)
-    add(4096 - 2 * size, even)
-    add(4096 - size, odd)
+    for k in range(1, chunks + 1):
+        if k < chunks:
+            collect(k * size, odd if k % 2 else even)
+        add((k - 1) * size, even if k % 2 else odd)
 
 
 def far_out(total, out_ref):
@@ -190,6 +181,7 @@
 
 MESH = pl.DeviceIdType.MESH
 GROUPS = 64
+SECOND = 5
 
 
 def each_other(g, skip, act, early=None):
@@ -289,13 +281,20 @@
     for load in loads:
         load.start()
 
-    @pl.when(s > 0)
-    def _():
-        pl.semaphore_signal(barrier, inc=1, device_id={"slab": s - 1}, device_id_type=MESH)
-
-    @pl.when(s < slabs - 1)
-    def _():
-        pl.semaphore_signal(barrier, inc=1, device_id={"slab": s + 1}, device_id_type=MESH)
+    def greet_slab(other):
+        pl.semaphore_signal(barrier, inc=1, device_id={"slab": other}, device_id_type=MESH)
+
+    upper = s < slabs - 1
+    upper_second = upper & (s < SECOND) & ((s > 0) | (g > 0))
+    is_second = (s > 0) & (s <= SECOND) & ((s > 1) | (g > 0))
+
+    @pl.when((s > 0) & jnp.logical_not(is_second))
+    def _():
+        greet_slab(s - 1)
+
+    @pl.when(upper & jnp.logical_not(upper_second))
+    def _():
+        greet_slab(s + 1)
 
     late = (s == 0) & (g == 0)
     meets_late = (s == 0) & (g != 0)
@@ -319,8 +318,16 @@
     own = window.at[4:8]
     own_window(coords, charges, stage, own)
 
-    inner = jnp.where(s > 0, 1, 0) + jnp.where(s < slabs - 1, 1, 0)
+    inner = jnp.where(s > 0, 1, 0) + jnp.where(upper & jnp.logical_not(upper_second), 1, 0)
     pl.semaphore_wait(barrier, GROUPS - 1 - jnp.where(meets_late, 1, 0) + inner)
+
+    @pl.when(upper_second)
+    def _():
+        greet_slab(s + 1)
+
+    @pl.when(is_second)
+    def _():
+        greet_slab(s - 1)
 
     @pl.when(meets_late)
     def _():
@@ -343,7 +350,7 @@
         device_id_type=MESH,
     )
 
-    @pl.when(s < slabs - 1)
+    @pl.when(upper & jnp.logical_not(upper_second))
     def _():
         up.start()
 
@@ -385,6 +392,11 @@
     target_table(entry_target, hot)
     near_table(window, cells, 1)
 
+    @pl.when(upper_second)
+    def _():
+        pl.semaphore_wait(barrier, 1)
+        up.start()
+
     @pl.when(s == 0)
     def _():
         window[0:4] = jnp.zeros((4, 64, 128), F32)
@@ -441,7 +453,7 @@
         start = pl.multiple_of(256 * k, 256)
         translate(received[pl.ds(start, 256), :], first, second, table, start)
 
-    collect_sum(index, table, hot, even, odd, total, 512)
+    collect_sum(index, table, hot, even, odd, total, 1024)
     far_out(total, far_rows)
 
     arrived(GROUPS - 1, 0).wait_send()
@@ -513,8 +525,8 @@
             vmem((4, 256, 128), BF16),
             vmem((8192, 128), F32),
             vmem((512, 4096), BF16),
-            vmem((512, 128), F32),
-            vmem((512, 128), F32),
+            vmem((1024, 128), F32),
+            vmem((1024, 128), F32),
             vmem((512, 256), F32),
             dma((10,)),
             dma((2,)),

time: 32 us -> 30.7 us (0.959)
  Pallas kernels: 29.9 us -> 28.6 us
    pallas_call x1, Pallas kernels: 29.9 us -> 28.6 us  [shards(): pl.pallas_call(kernel, out_shape=[vmem((121, 512), F32), vmem((64, 128),...]
where the time goes in v6:
time: 30.7 us; the launch traced here: 30.6 us
  Pallas kernels  28.6 us (93%)
  local copies, waits for them, and re-layouts  1.32 us (4%)
  between operations  0.64 us (2%)
    pallas_call x1, Pallas kernels, shards(): pl.pallas_call(kernel, out_shape=[vmem((121, 512), F32), vmem((64, 128),...  28.6 us
    unnamed x2, local copies, waits for them, and re-layouts  1.32 us

profile of v6, /device:TPU:192, one launch (start us, length us, event | category | flops | bytes accessed | tf_op | source)
XLA Modules:
  0.0 30.6 jit_solution(3516043464386061576)
XLA Ops:
  0.6 28.6 %shard_map.104 = (f32[121,512]{1,0:T(8,128)S(1)}, f32[64,128]{1,0:T(8,128)S(1)}) custom-call(f32[3,8192]{1,0:T(4,128)} %coords_hbm.1, f32[64,128]{1,0:T(8,128)} %bitcast.6, f32[121,512]{1,0:T(8,128)} %mult_hbm.1, f32[121,8,121]{2,1,0:T(8,128)} %bitcast.5, s32[1,1024]{1,0:T(1,128)} %send_hbm.1, s32[8,512]{1,0:T(8,128)} %bitcast.7, s32[1,4096]{1,0:T(1,128)} %source_hbm.1, ...), custom_call_target="tpu_custom_call" | custom-call | tf_op jit(solution)/shard_map/pallas_call | solution.py:494
  29.2 0.7 %copy.13 = f32[121,512]{1,0:T(8,128)} copy(f32[121,512]{1,0:T(8,128)S(1)} %get-tuple-element.6) | data formatting | bytes 495616
  29.9 0.6 %copy.14 = f32[8192]{0:T(1024)} copy(f32[8192]{0:T(1024)S(1)} %bitcast.4) | data formatting | bytes 65536
